TPU v7x, 32 devices: a whole 2x2x4 slice. The times are simulated.
32 devices in a mesh: fsdp: 8 (over z, x), tp: 4 (over y, core).
Axes of the slice: x: 2, y: 2, z: 4, core: 2. Of those that a mesh axis runs over, the one named last changes fastest.
Arguments:
- grad_out: bfloat16 [2048, 8192], P('fsdp', 'tp'), may hold values from -6 to 6
- down_q: bfloat16 [14336, 8192], P('fsdp', 'tp'), may hold values from -0.0625 to 0.0625
- scales: bfloat16 [112, 64], P('fsdp', 'tp'), may hold values from 0.25 to 4
- gate_act: bfloat16 [2048, 14336], P('fsdp', 'tp'), may hold values from -6 to 6
- up_act: bfloat16 [2048, 14336], P('fsdp', 'tp'), may hold values from -6 to 6
Outputs:
- grad_gate: bfloat16 [2048, 14336], P('fsdp', 'tp')
- grad_up: bfloat16 [2048, 14336], P('fsdp', 'tp')
All inputs are finite; a program needn't handle non-finite values.
Results may differ from a plain program's by a relative error of at most 0.005.
Values may be sent and summed in bfloat16 or wider, within the bound.
A program may use at most 192 MiB of HBM per device.

v0:
```python
import jax
import jax.numpy as jnp
from jax import lax
from jax.sharding import PartitionSpec as P

BLOCK = 128


def dequantize(blocks, scales):
    count, height, width = blocks.shape
    grid = blocks.astype(jnp.float32).reshape(count, height, width // BLOCK, BLOCK)
    grid = grid * scales.astype(jnp.float32)[:, None, :, None]
    return grid.reshape(count, height, width).astype(jnp.bfloat16)


def on_device(grad_out, down_q, scales, gate_act, up_act):
    columns = grad_out.shape[1]
    blocks = down_q.reshape(-1, BLOCK, columns)
    flat = dequantize(
        lax.all_gather(blocks, "fsdp", axis=0, tiled=True),
        lax.all_gather(scales, "fsdp", axis=0, tiled=True),
    ).reshape(-1, columns)
    partial_value = lax.dot_general(
        grad_out, flat, (((1,), (1,)), ((), ())), preferred_element_type=jnp.float32
    )
    grad_hidden = lax.psum_scatter(partial_value, "tp", scatter_dimension=1, tiled=True)
    gate_val = gate_act.astype(jnp.float32)
    sigmoid_gate = jax.nn.sigmoid(gate_val)
    grad_up = (grad_hidden * gate_val * sigmoid_gate).astype(jnp.bfloat16)
    slope = sigmoid_gate * (1.0 + gate_val * (1.0 - sigmoid_gate))
    grad_gate = (grad_hidden * up_act.astype(jnp.float32) * slope).astype(jnp.bfloat16)
    return (grad_gate, grad_up)


def solution(mesh):
    return jax.shard_map(
        on_device,
        mesh=mesh,
        in_specs=(
            P("fsdp", "tp"),
            P("fsdp", "tp"),
            P("fsdp", "tp"),
            P("fsdp", "tp"),
            P("fsdp", "tp"),
        ),
        out_specs=(P("fsdp", "tp"), P("fsdp", "tp")),
        check_vma=False,
    )
```

profile of v0, /device:TPU:24, one launch (start us, length us, event | category | flops | bytes accessed | tf_op | source)
XLA Modules:
  0.0 1318.9 jit_solution(193647179098432543)
XLA Ops:
  7.2 0.0 copy-start
  7.2 0.0 all-gather.3.cloned.1.call-start
  7.2 0.0 copy-start.3
  7.2 0.7 all-gather.3.cloned.1.call-update
  7.9 0.0 reduce-scatter.2.cloned.1.call-start
  8.0 0.0 copy-done.3
  8.0 102.4 %all-gather = bf16[8,14,16]{2,1,0:T(8,128)(2,1)S(1)} all-gather(bf16[1,14,16]{2,1,0:T(8,128)(2,1)S(1)} %bitcast.15), channel_id=1, replica_groups=mesh['fsdp'=8,'tp'=4] {'fsdp'}, dimensions={0}, use_global_device_ids=true | all-gather | bytes 4032 | tf_op jit(solution)/shard_map/all_gather | solution.py:21
  110.4 0.3 mul.31
  110.7 0.3 copy.35
  111.0 1009.5 %all-gather.3.cloned.1.call-done = bf16[112,128,2048]{2,1,0:T(8,128)(2,1)} async-done(((bf16[14,128,2048]{2,1,0:T(8,128)(2,1)}), bf16[112,128,2048]{2,1,0:T(8,128)(2,1)}) %all-gather.3.cloned.1.call-update) | async-done | bytes 58720272 | tf_op jit(solution)/shard_map/all_gather | solution.py:20
  1120.5 39.0 %multiply_convert_fusion = bf16[112,128,2048]{2,1,0:T(8,128)(2,1)} fusion(bf16[112,128,2048]{2,1,0:T(8,128)(2,1)} %all-gather.3.cloned.1.call-done, f32[112,2048]{1,0:T(8,128)S(1)} %bitcast.14), kind=kLoop, calls=%fused_computation | loop fusion | flops 88080384 | bytes 118358016 | tf_op jit(solution)/shard_map/convert_element_type | solution.py:13
  1159.6 0.0 copy-done
  1159.6 28.0 %convolution_bitcast_fusion = f32[256,14336]{0,1:T(8,128)} fusion(bf16[14336,2048]{1,0:T(8,128)(2,1)} %bitcast.11, bf16[256,2048]{1,0:T(8,128)(2,1)S(1)} %copy-done), kind=kOutput, calls=%fused_computation.1 | convolution fusion | flops 15032385536 | bytes 74448896 | tf_op jit(solution)/shard_map/dot_general | solution.py:23
  1187.6 0.0 reduce-scatter.2.cloned.1.call-update
  1187.7 2.9 copy.27
  1190.6 3.8 copy.26
  1194.4 106.4 %reduce-scatter.2.cloned.1.call-done = f32[256,3584]{0,1:T(8,128)} async-done(((f32[256,14336]{0,1:T(8,128)}), f32[256,3584]{0,1:T(8,128)}) %reduce-scatter.2.cloned.1.call-update) | async-done | bytes 3670032 | tf_op jit(solution)/shard_map/reduce_scatter | solution.py:26
  1300.8 4.8 fusion.8
  1305.6 0.0 copy-start.2
  1305.6 0.0 copy-start.1
  1305.6 4.0 copy.29
  1309.5 0.0 copy-done.2
  1309.6 2.5 copy.28
  1312.1 0.0 copy-done.1
  (3 shorter events, 0.0 us)
Async XLA Ops:
  7.2 1152.4 %copy-start = (bf16[256,2048]{1,0:T(8,128)(2,1)S(1)}, bf16[256,2048]{1,0:T(8,128)(2,1)}, u32[]{:S(2)}) copy-start(bf16[256,2048]{1,0:T(8,128)(2,1)} %param.5) | copy-start | bytes 3145732
  7.2 1113.4 %all-gather.3.cloned.1.call-start = ((), (), s32[]{:S(2)}) async-start(), calls=%async_computation.1 | async-start | bytes 66060288 | tf_op jit(solution)/shard_map/all_gather | solution.py:20
  7.2 0.8 copy-start.3
  7.9 1292.9 %reduce-scatter.2.cloned.1.call-start = ((), (), s32[]{:S(2)}) async-start(), calls=%async_computation.2 | async-start | bytes 18350080 | tf_op jit(solution)/shard_map/reduce_scatter | solution.py:26
  1305.6 4.0 copy-start.2
  1305.6 6.5 copy-start.1
Sparse Core Ops, SparseCore 0:
  9.5 1110.9 all-gather.2
  1187.8 112.9 reduce-scatter.1
where the time goes:
time: 1320 us
  waiting for transfers between devices  1120 us (85%)
  blocking collectives  102 us (8%)
  other arithmetic  43.9 us (3%)
  matrix products  28 us (2%)
  between operations  14.1 us (1%)
  local copies, waits for them, and re-layouts  13.8 us (1%)
    all_gather x1, waiting for transfers between devices, on_device(): lax.all_gather(blocks, 'fsdp', axis=0, tiled=True)  1010 us
    reduce_scatter x1, waiting for transfers between devices, on_device(): lax.psum_scatter(partial_value, 'tp', scatter_dimension=1, tiled=True)  106 us
    all_gather x1, blocking collectives, on_device(): lax.all_gather(scales, 'fsdp', axis=0, tiled=True)  102 us
    convert_element_type x1, other arithmetic, dequantize(): return grid.reshape(count, height, width).astype(jnp.bfloat16)  39 us
    dot_general x1, matrix products, on_device(): lax.dot_general(grad_out, flat, (((1,), (1,)), ((), ())), preferred_eleme...  28 us
  transfers between devices with their start and end apart: 2, of which 2 were waited for; matrix products, arithmetic and copies ran while one was open for 1% of the time, Pallas kernels for 0%

commit v1 on v0

v1 whole, which is shorter than its diff:
```python
import jax
import jax.numpy as jnp
from jax import lax
from jax.sharding import PartitionSpec as P

BLOCK = 128


def dequantize(values, scales):
    rows, cols = values.shape
    grid = values.astype(jnp.float32).reshape(rows // BLOCK, BLOCK, cols // BLOCK, BLOCK)
    grid = grid * scales.astype(jnp.float32)[:, None, :, None]
    return grid.reshape(rows, cols).astype(jnp.bfloat16)


def on_device(F, T, grad_out, down_q, scales, gate_act, up_act):
    R = F // T
    f = lax.axis_index("fsdp")
    rows = grad_out.shape[0]
    hidden = down_q.shape[0]
    weight = dequantize(down_q, scales)
    tokens = lax.all_gather(grad_out, "fsdp", axis=0, tiled=True)
    partial_value = lax.dot_general(
        tokens, weight, (((1,), (1,)), ((), ())), preferred_element_type=jnp.float32
    ).astype(jnp.bfloat16)
    mine = lax.psum_scatter(partial_value, "tp", scatter_dimension=0, tiled=True)
    mine = mine.reshape(R, rows, hidden)
    own_f = lax.axis_index("fsdp")
    grad_hidden = jnp.zeros((rows, R, hidden), jnp.bfloat16)
    for s in range(R):
        pairs = []
        for a in range(F):
            for b in range(T):
                j = (a + s) % R
                pairs.append((a * T + b, (R * b + j) * T + a // R))
        piece = lax.dynamic_index_in_dim(mine, (own_f + s) % R, 0, keepdims=False)
        got = lax.ppermute(piece, ("fsdp", "tp"), pairs)
        i = (own_f - s) % R
        grad_hidden = lax.dynamic_update_slice(grad_hidden, got[:, None, :], (0, i, 0))
    grad_hidden = grad_hidden.reshape(rows, R * hidden).astype(jnp.float32)
    gate_val = gate_act.astype(jnp.float32)
    sigmoid_gate = jax.nn.sigmoid(gate_val)
    grad_up = (grad_hidden * gate_val * sigmoid_gate).astype(jnp.bfloat16)
    slope = sigmoid_gate * (1.0 + gate_val * (1.0 - sigmoid_gate))
    grad_gate = (grad_hidden * up_act.astype(jnp.float32) * slope).astype(jnp.bfloat16)
    return (grad_gate, grad_up)


def solution(mesh):
    F, T = mesh.shape["fsdp"], mesh.shape["tp"]

    def body(*args):
        return on_device(F, T, *args)

    spec = P("fsdp", "tp")
    return jax.shard_map(
        body, mesh=mesh, in_specs=(spec,) * 5, out_specs=(spec, spec), check_vma=False
    )
```

time: 1320 us -> 404 us (0.31)
  the two profiles are of different devices: /device:TPU:24 before, /device:TPU:4 now
where the time goes in v1:
time: 404 us; the launch traced here: 398 us
  waiting for transfers between devices  268 us (66%)
  local copies, waits for them, and re-layouts  78.9 us (20%)
  matrix products  26.8 us (7%)
  between operations  14.1 us (3%)
  starting transfers between devices  7.18 us (2%)
    all_gather x1, waiting for transfers between devices, on_device(): tokens = lax.all_gather(grad_out, 'fsdp', axis=0, tiled=True)  128 us
    ppermute x2, waiting for transfers between devices, on_device(): got = lax.ppermute(piece, ('fsdp', 'tp'), pairs)  76.2 us
    reduce_scatter x1, waiting for transfers between devices, on_device(): lax.psum_scatter(partial_value, 'tp', scatter_dimension=0, tiled=True)  62.6 us
    dynamic_update_slice x2, local copies, waits for them, and re-layouts, on_device(): lax.dynamic_update_slice(grad_hidden, got[:, None, :], (0, i, 0))  56.1 us
    dot_general x1, matrix products, on_device(): lax.dot_general(tokens, weight, (((1,), (1,)), ((), ())), preferred_eleme...  26.8 us
  transfers between devices with their start and end apart: 4, of which 4 were waited for; matrix products, arithmetic and copies ran while one was open for 1% of the time, Pallas kernels for 0%

profile of v1, /device:TPU:4, one launch (start us, length us, event | category | flops | bytes accessed | tf_op | source)
XLA Modules:
  0.0 397.9 jit_solution(10575064398277431266)
XLA Ops:
  7.2 0.0 all-gather.2.cloned.1.call-start
  7.2 0.7 all-gather.2.cloned.1.call-update
  7.9 0.0 reduce-scatter.2.cloned.1.call-start
  7.9 128.3 %all-gather.2.cloned.1.call-done = bf16[2048,2048]{1,0:T(8,128)(2,1)} async-done(((bf16[256,2048]{1,0:T(8,128)(2,1)}), bf16[2048,2048]{1,0:T(8,128)(2,1)}) %all-gather.2.cloned.1.call-update) | async-done | bytes 8388624 | tf_op jit(solution)/shard_map/all_gather | solution.py:22
  136.3 6.9 %mul.29 = f32[14,128,16,128]{3,2,1,0:T(8,128)} broadcast(bf16[14,16]{1,0:T(8,128)(2,1)} %param.7), dimensions={0,2} | broadcast | bytes 14680512 | tf_op jit(solution)/shard_map/mul | solution.py:12
  143.2 26.8 %fusion.2 = bf16[2048,1792]{0,1:T(8,128)(2,1)} fusion(bf16[2048,2048]{1,0:T(8,128)(2,1)} %all-gather.2.cloned.1.call-done, f32[224,8,16,128]{3,2,1,0:T(8,128)} %bitcast.22, bf16[1792,2048]{1,0:T(8,128)(2,1)} %param.6), kind=kOutput, calls=%fused_computation.3 | convolution fusion | flops 15047065600 | bytes 37748736 | tf_op jit(solution)/shard_map/dot_general | solution.py:23
  170.0 0.0 reduce-scatter.2.cloned.1.call-update
  170.0 62.6 %reduce-scatter.2.cloned.1.call-done = bf16[512,1792]{0,1:T(8,128)(2,1)} async-done(((bf16[2048,1792]{0,1:T(8,128)(2,1)}), bf16[512,1792]{0,1:T(8,128)(2,1)}) %reduce-scatter.2.cloned.1.call-update) | async-done | bytes 1835024 | tf_op jit(solution)/shard_map/reduce_scatter | solution.py:26
  232.6 2.8 copy.11
  235.4 1.1 dynamic-slice_bitcast_fusion
  236.5 5.6 %collective-permute-start = (bf16[256,1792]{1,0:T(8,128)(2,1)}, bf16[256,1792]{1,0:T(8,128)(2,1)S(1)}, u32[]{:S(2)}, u32[]{:S(2)}) collective-permute-start(bf16[256,1792]{1,0:T(8,128)(2,1)} %get-tuple-element.5), channel_id=1, source_target_pairs={{0,0},{1,8},{2,16},{3,24},{4,4},{5,12},{6,20},{7,28},{8,1},{9,9},{... | collective-permute-start | bytes 2752520 | tf_op jit(solution)/shard_map/ppermute | solution.py:37
  242.1 1.5 collective-permute-start.1
  243.6 59.3 %collective-permute-done = bf16[256,1792]{1,0:T(8,128)(2,1)S(1)} collective-permute-done((bf16[256,1792]{1,0:T(8,128)(2,1)}, bf16[256,1792]{1,0:T(8,128)(2,1)S(1)}, u32[]{:S(2)}, u32[]{:S(2)}) %collective-permute-start) | collective-permute-done | bytes 917536 | tf_op jit(solution)/shard_map/ppermute | solution.py:37
  302.9 0.0 copy-start.2
  302.9 0.9 copy-done.2
  303.8 2.6 copy.8
  306.4 16.8 %collective-permute-done.1 = bf16[256,1792]{1,0:T(8,128)(2,1)} collective-permute-done((bf16[256,1792]{1,0:T(8,128)(2,1)S(1)}, bf16[256,1792]{1,0:T(8,128)(2,1)}, u32[]{:S(2)}, u32[]{:S(2)}) %collective-permute-start.1) | collective-permute-done | bytes 917536 | tf_op jit(solution)/shard_map/ppermute | solution.py:37
  323.3 3.8 copy.10
  327.1 2.2 broadcast_in_dim.10
  329.3 27.9 %dynamic_update_slice.6 = bf16[256,2,1792]{2,1,0:T(2,128)(2,1)} dynamic-update-slice(bf16[256,2,1792]{2,1,0:T(2,128)(2,1)} %broadcast_in_dim.10, bf16[256,1,1792]{2,1,0:T(2,128)(2,1)S(1)} %copy.8, s32[]{:T(128)} %constant.38.clone.1, s32[]{:T(128)S(6)} %select_n.29, s32[]{:T(128)} %constant.38.clone.1) | dynamic-update-slice | bytes 1835012 | tf_op jit(solution)/shard_map/dynamic_update_slice | solution.py:39
  357.1 28.3 %dynamic_update_slice.7 = bf16[256,2,1792]{2,1,0:T(2,128)(2,1)} dynamic-update-slice(bf16[256,2,1792]{2,1,0:T(2,128)(2,1)} %dynamic_update_slice.6, bf16[256,1,1792]{2,1,0:T(2,128)(2,1)} %copy.10, s32[]{:T(128)} %constant.38.clone.1, s32[]{:T(128)S(6)} %select_n.33, s32[]{:T(128)} %constant.38.clone.1) | dynamic-update-slice | bytes 1835012 | tf_op jit(solution)/shard_map/dynamic_update_slice | solution.py:39
  385.4 0.0 copy-start
  385.4 0.0 copy-start.1
  385.4 2.1 copy.13
  387.5 0.0 copy-done
  387.5 0.5 copy-done.1
  388.0 3.0 fusion.13
Async XLA Ops:
  7.2 129.1 %all-gather.2.cloned.1.call-start = ((), (), s32[]{:S(2)}) async-start(), calls=%async_computation.1 | async-start | bytes 9437184 | tf_op jit(solution)/shard_map/all_gather | solution.py:22
  7.9 224.7 %reduce-scatter.2.cloned.1.call-start = ((), (), s32[]{:S(2)}) async-start(), calls=%async_computation.2 | async-start | bytes 9175040 | tf_op jit(solution)/shard_map/reduce_scatter | solution.py:26
  236.5 66.4 %collective-permute-start = (bf16[256,1792]{1,0:T(8,128)(2,1)}, bf16[256,1792]{1,0:T(8,128)(2,1)S(1)}, u32[]{:S(2)}, u32[]{:S(2)}) collective-permute-start(bf16[256,1792]{1,0:T(8,128)(2,1)} %get-tuple-element.5), channel_id=1, source_target_pairs={{0,0},{1,8},{2,16},{3,24},{4,4},{5,12},{6,20},{7,28},{8,1},{9,9},{... | collective-permute-start | bytes 2752520 | tf_op jit(solution)/shard_map/ppermute | solution.py:37
  242.1 81.1 %collective-permute-start.1 = (bf16[256,1792]{1,0:T(8,128)(2,1)S(1)}, bf16[256,1792]{1,0:T(8,128)(2,1)}, u32[]{:S(2)}, u32[]{:S(2)}) collective-permute-start(bf16[256,1792]{1,0:T(8,128)(2,1)S(1)} %get-tuple-element.4), channel_id=1, source_target_pairs={{0,4},{1,12},{2,20},{3,28},{4,0},{5,8},{6,16},{7,24},{8,5},{9,13},... | collective-permute-start | bytes 2752520 | tf_op jit(solution)/shard_map/ppermute | solution.py:37
  302.9 0.9 copy-start.2
  385.4 2.1 copy-start
  385.4 2.6 copy-start.1
Sparse Core Ops, SparseCore 0:
  10.1 126.1 all-gather.1
  170.1 62.4 reduce-scatter.1

commit v2 on v0

v2 whole, which is shorter than its diff:
```python
import functools

import jax
import jax.numpy as jnp
from jax import lax
from jax.experimental import pallas as pl
from jax.experimental.pallas import tpu as pltpu
from jax.sharding import PartitionSpec as P

BLOCK = 128
X = 2
LAG_X = 2
LAG_SUM = 2
MESH = pl.DeviceIdType.MESH


def kernel(F, T, a_ref, q_ref, s_ref, out_ref, ga, w, part, tile, acc, rbuf, fin,
           lsem, gr, up, dn, xs, ts, tr, fs, fr):
    R, Z = F // T, F // X
    tb = a_ref.shape[0]
    hb = q_ref.shape[0]
    pb = tb // T
    wide = 256 if hb % 256 == 0 else 128
    f, t = lax.axis_index("fsdp"), lax.axis_index("tp")
    z, x = lax.div(f, X), lax.rem(f, X)
    xpeer = f + 1 - 2 * x
    owner_t, owner_i = lax.div(f, R), lax.rem(f, R)
    to_self = owner_t == t

    copy_a = pltpu.make_async_copy(a_ref, ga.at[f], lsem.at[0])
    copy_q = pltpu.make_async_copy(q_ref, w, lsem.at[1])
    copy_a.start()
    copy_q.start()

    barrier = pltpu.get_barrier_semaphore()

    def greet(df, dt):
        pl.semaphore_signal(barrier, inc=1, device_id=(df, dt), device_id_type=MESH)

    @pl.when(z > 0)
    def _():
        greet(f - X, t)

    @pl.when(z < Z - 1)
    def _():
        greet(f + X, t)

    greet(xpeer, t)
    for o in range(1, T):
        greet(f, lax.rem(t + o, T))

    for i in range(R):
        @pl.loop(0, T)
        def _(t2):
            @pl.when(jnp.logical_not((t * R + i == f) & (t2 == t)))
            def _():
                greet(t * R + i, t2)

    waits = 1 + (T - 1) + F
    waits = waits + (z > 0).astype(jnp.int32) + (z < Z - 1).astype(jnp.int32)
    pl.semaphore_wait(barrier, waits - to_self.astype(jnp.int32))

    def gather_copy(zz, sem, df):
        slot = zz * X + x
        return pltpu.make_async_remote_copy(
            src_ref=ga.at[slot], dst_ref=ga.at[slot], send_sem=sem.at[zz],
            recv_sem=gr.at[slot], device_id=(df, t), device_id_type=MESH)

    def gather_recv(slot):
        pltpu.make_async_remote_copy(
            src_ref=ga.at[slot], dst_ref=ga.at[slot], send_sem=xs.at[0],
            recv_sem=gr.at[slot], device_id=(xpeer, t), device_id_type=MESH).wait_recv()

    def forward(zz, act):
        @pl.when((zz <= z) & (z < Z - 1))
        def _():
            act(gather_copy(zz, up, f + X))

        @pl.when((zz >= z) & (z > 0))
        def _():
            act(gather_copy(zz, dn, f - X))

        act(gather_copy(zz, xs, xpeer))

    def tp_copy(slot, t2):
        return pltpu.make_async_remote_copy(
            src_ref=part.at[slot, pl.ds(pl.multiple_of(t2 * pb, pb), pb), :],
            dst_ref=rbuf.at[slot, t], send_sem=ts.at[slot, t2],
            recv_sem=tr.at[slot, t], device_id=(f, t2), device_id_type=MESH)

    def tp_recv(slot, t2):
        pltpu.make_async_remote_copy(
            src_ref=rbuf.at[slot, t2], dst_ref=rbuf.at[slot, t2], send_sem=ts.at[slot, t2],
            recv_sem=tr.at[slot, t2], device_id=(f, t2), device_id_type=MESH).wait_recv()

    def out_at(i, t2):
        return out_ref.at[pl.ds(pl.multiple_of(t2 * pb, pb), pb),
                          pl.ds(pl.multiple_of(i * hb, 128), hb)]

    def fin_remote(slot):
        return pltpu.make_async_remote_copy(
            src_ref=fin.at[slot], dst_ref=out_at(owner_i, t), send_sem=fs.at[slot],
            recv_sem=fr.at[owner_i, t], device_id=(slot, owner_t), device_id_type=MESH)

    def fin_local():
        return pltpu.make_async_copy(fin.at[f], out_at(owner_i, t), lsem.at[2])

    def multiply(slot):
        @pl.loop(0, hb // wide)
        def _(n):
            at = pl.ds(pl.multiple_of(n * wide, wide), wide)
            prod = lax.dot_general(ga[slot], w[at, :], (((1,), (1,)), ((), ())),
                                   preferred_element_type=jnp.float32)
            tile[:, at] = prod
            part[slot, :, at] = prod.astype(jnp.bfloat16)

        acc[slot] = tile[pl.ds(pl.multiple_of(t * pb, pb), pb), :]
        for o in range(1, T):
            tp_copy(slot, lax.rem(t + o, T)).start()

    def add_up(slot):
        for o in range(1, T):
            tp_recv(slot, lax.rem(t + o, T))
        total = acc[slot]
        for o in range(1, T):
            total = total + rbuf[slot, lax.rem(t + o, T)].astype(jnp.float32)
        fin[slot] = total.astype(jnp.bfloat16)
        own = to_self & (slot == f)

        @pl.when(own)
        def _():
            fin_local().start()

        @pl.when(jnp.logical_not(own))
        def _():
            fin_remote(slot).start()

    copy_a.wait()
    forward(z, lambda c: c.start())
    copy_q.wait()

    @pl.loop(0, hb // BLOCK)
    def _(b):
        at = pl.ds(pl.multiple_of(b * BLOCK, BLOCK), BLOCK)
        w[at, :] = (w[at, :].astype(jnp.float32) * s_ref[pl.ds(b, 1), :]).astype(jnp.bfloat16)

    steps = 2 * Z - 1

    def when_valid(k, body):
        d = lax.div(k + 1, 2)
        zz = z + d * (1 - 2 * lax.rem(k, 2))

        @pl.when((k >= 0) & (k < steps) & (zz >= 0) & (zz < Z))
        def _():
            body(zz)

    def own_column(zz):
        slot = zz * X + x

        @pl.when(zz != z)
        def _():
            gather_recv(slot)
            forward(zz, lambda c: c.start())

        multiply(slot)

    def other_column(zz):
        slot = zz * X + 1 - x
        gather_recv(slot)
        multiply(slot)

    @pl.loop(0, steps + LAG_X + LAG_SUM)
    def _(i):
        when_valid(i, own_column)
        when_valid(i - LAG_SUM, lambda zz: add_up(zz * X + x))
        when_valid(i - LAG_X, other_column)
        when_valid(i - LAG_X - LAG_SUM, lambda zz: add_up(zz * X + 1 - x))

    @pl.loop(0, Z)
    def _(zz):
        forward(zz, lambda c: c.wait_send())

    @pl.loop(0, F)
    def _(slot):
        for o in range(1, T):
            tp_copy(slot, lax.rem(t + o, T)).wait_send()
        own = to_self & (slot == f)

        @pl.when(own)
        def _():
            fin_local().wait()

        @pl.when(jnp.logical_not(own))
        def _():
            fin_remote(slot).wait_send()

    for i in range(R):
        @pl.loop(0, T)
        def _(t2):
            @pl.when(jnp.logical_not((t * R + i == f) & (t2 == t)))
            def _():
                pltpu.make_async_remote_copy(
                    src_ref=fin.at[0], dst_ref=out_at(i, t2), send_sem=fs.at[0],
                    recv_sem=fr.at[i, t2], device_id=(t * R + i, t2),
                    device_id_type=MESH).wait_recv()


def hidden_gradient(F, T, grad_out, down_q, scales):
    R, Z = F // T, F // X
    tb, kd = grad_out.shape
    hb = down_q.shape[0]
    pb = tb // T
    wide_scales = jnp.repeat(scales.astype(jnp.float32), BLOCK, axis=1)
    any_spec = pl.BlockSpec(memory_space=pl.ANY)
    return pl.pallas_call(
        functools.partial(kernel, F, T),
        out_shape=jax.ShapeDtypeStruct((tb, R * hb), jnp.bfloat16),
        in_specs=[any_spec, any_spec, pl.BlockSpec(memory_space=pltpu.VMEM)],
        out_specs=any_spec,
        scratch_shapes=[
            pltpu.VMEM((F, tb, kd), jnp.bfloat16),
            pltpu.VMEM((hb, kd), jnp.bfloat16),
            pltpu.VMEM((F, tb, hb), jnp.bfloat16),
            pltpu.VMEM((tb, hb), jnp.float32),
            pltpu.VMEM((F, pb, hb), jnp.float32),
            pltpu.VMEM((F, T, pb, hb), jnp.bfloat16),
            pltpu.VMEM((F, pb, hb), jnp.bfloat16),
            pltpu.SemaphoreType.DMA((3,)),
            pltpu.SemaphoreType.DMA((F,)),
            pltpu.SemaphoreType.DMA((Z,)),
            pltpu.SemaphoreType.DMA((Z,)),
            pltpu.SemaphoreType.DMA((Z,)),
            pltpu.SemaphoreType.DMA((F, T)),
            pltpu.SemaphoreType.DMA((F, T)),
            pltpu.SemaphoreType.DMA((F,)),
            pltpu.SemaphoreType.DMA((R, T)),
        ],
        compiler_params=pltpu.CompilerParams(
            collective_id=0, has_side_effects=True, vmem_limit_bytes=56 * 2**20),
        cost_estimate=pl.CostEstimate(
            flops=2 * F * tb * kd * hb, bytes_accessed=2 * hb * (kd + R * tb),
            transcendentals=0),
    )(grad_out, down_q, wide_scales)


def on_device(F, T, grad_out, down_q, scales, gate_act, up_act):
    grad_hidden = hidden_gradient(F, T, grad_out, down_q, scales).astype(jnp.float32)
    gate_val = gate_act.astype(jnp.float32)
    sigmoid_gate = jax.nn.sigmoid(gate_val)
    grad_up = (grad_hidden * gate_val * sigmoid_gate).astype(jnp.bfloat16)
    slope = sigmoid_gate * (1.0 + gate_val * (1.0 - sigmoid_gate))
    grad_gate = (grad_hidden * up_act.astype(jnp.float32) * slope).astype(jnp.bfloat16)
    return (grad_gate, grad_up)


def solution(mesh):
    F, T = mesh.shape["fsdp"], mesh.shape["tp"]
    spec = P("fsdp", "tp")
    return jax.shard_map(
        functools.partial(on_device, F, T),
        mesh=mesh, in_specs=(spec,) * 5, out_specs=(spec, spec), check_vma=False)
```

time: 1320 us -> 149 us (0.11)
  waiting for transfers between devices: 1120 us -> 0 us
  Pallas kernels: 0 us -> 142 us
  blocking collectives: 102 us -> 0 us
  other arithmetic: 43.9 us -> 4.33 us
  matrix products: 28 us -> 0 us
  between operations: 14.1 us -> 0.67 us
    all_gather x1 -> x0, waiting for transfers between devices: 1010 us -> none  [on_device(): lax.all_gather(blocks, 'fsdp', axis=0, tiled=True)]
    pallas_call x0 -> x1, Pallas kernels: none -> 142 us  [hidden_gradient(): pl.pallas_call(functools.partial(kernel, F, T), out_shape=jax.ShapeDtypeS...]
    reduce_scatter x1 -> x0, waiting for transfers between devices: 106 us -> none  [on_device(): lax.psum_scatter(partial_value, 'tp', scatter_dimension=1, tiled=True)]
    all_gather x1 -> x0, blocking collectives: 102 us -> none  [on_device(): lax.all_gather(scales, 'fsdp', axis=0, tiled=True)]
    convert_element_type x2 -> x0, other arithmetic: 39.1 us -> none  [the longest x1 39 us: dequantize(): return grid.reshape(count, height, width).astype(jnp.bfloat16)]
    dot_general x1 -> x0, matrix products: 28 us -> none  [on_device(): lax.dot_general(grad_out, flat, (((1,), (1,)), ((), ())), preferred_eleme...]
  transfers between devices with their start and end apart: 2 -> 0, of which waited for: 2 -> 0; matrix products, arithmetic and copies ran while one was open for 1% -> 0% of each run, Pallas kernels for 0% -> 0%
where the time goes in v2:
time: 149 us
  Pallas kernels  142 us (95%)
  other arithmetic  4.33 us (3%)
  local copies, waits for them, and re-layouts  1.49 us (1%)
    pallas_call x1, Pallas kernels, hidden_gradient(): pl.pallas_call(functools.partial(kernel, F, T), out_shape=jax.ShapeDtypeS...  142 us
    convert_element_type x1, other arithmetic, on_device(): grad_up = (grad_hidden * gate_val * sigmoid_gate).astype(jnp.bfloat16)  4.33 us

profile of v2, /device:TPU:24, one launch (start us, length us, event | category | flops | bytes accessed | tf_op | source)
XLA Modules:
  0.0 149.0 jit_solution(2856606180809068346)
XLA Ops:
  0.6 0.8 broadcast_in_dim.3
  1.4 0.7 copy.7
  2.1 0.0 copy-start
  2.1 0.0 copy-start.1
  2.1 142.5 %shard_map.68 = bf16[256,3584]{1,0:T(8,128)(2,1)} custom-call(bf16[256,2048]{1,0:T(8,128)(2,1)} %a_ref.1, bf16[1792,2048]{1,0:T(8,128)(2,1)} %q_ref.1, f32[14,2048]{1,0:T(8,128)} %bitcast.4), custom_call_target="tpu_custom_call" | custom-call | flops 15032385536 | bytes 9175040 | tf_op jit(solution)/shard_map/pallas_call | solution.py:215
  144.6 0.0 copy-done
  144.6 0.0 copy-done.1
  144.6 4.3 %fusion.8 = (bf16[256,3584]{1,0:T(8,128)(2,1)}, bf16[256,3584]{1,0:T(8,128)(2,1)}) fusion(bf16[256,3584]{1,0:T(8,128)(2,1)S(1)} %copy-done, bf16[256,3584]{1,0:T(8,128)(2,1)} %shard_map.68, bf16[256,3584]{1,0:T(8,128)(2,1)S(1)} %copy-done.1), kind=kLoop, calls=%fused_computation.12 | loop fusion | flops 14680064 | bytes 9175040 | tf_op jit(solution)/shard_map/convert_element_type | solution.py:250
  (1 shorter events, 0.0 us)
Async XLA Ops:
  2.1 142.5 %copy-start = (bf16[256,3584]{1,0:T(8,128)(2,1)S(1)}, bf16[256,3584]{1,0:T(8,128)(2,1)}, u32[]{:S(2)}) copy-start(bf16[256,3584]{1,0:T(8,128)(2,1)} %param.8) | copy-start | bytes 5505028
  2.1 142.5 %copy-start.1 = (bf16[256,3584]{1,0:T(8,128)(2,1)S(1)}, bf16[256,3584]{1,0:T(8,128)(2,1)}, u32[]{:S(2)}) copy-start(bf16[256,3584]{1,0:T(8,128)(2,1)} %param.9) | copy-start | bytes 5505028

commit v3 on v2

v3 whole, which is shorter than its diff:
```python
import functools
import math

import jax
import jax.numpy as jnp
from jax import lax
from jax.experimental import pallas as pl
from jax.experimental.pallas import tpu as pltpu
from jax.sharding import PartitionSpec as P

BLOCK = 128
X = 2
CORES = 2
CHUNKS = 2
LAG_X = 3
LAG_SUM = 2
MESH = pl.DeviceIdType.MESH


def kernel(F, T, aligned, a_ref, q_ref, s_ref, out_ref, ga, q, w, part, tile, acc, rbuf, fin,
           lsem, wsem, gr, up, dn, xs, sr, ss, ts, tr, fs, fr):
    R, Z, U = F // T, F // X, T // CORES
    tb, kd = a_ref.shape
    hb = q_ref.shape[0]
    hh = hb // CORES
    pb, cb = tb // U, tb // CHUNKS
    f, t = lax.axis_index("fsdp"), lax.axis_index("tp")
    z, x = lax.div(f, X), lax.rem(f, X)
    u, c = lax.div(t, CORES), lax.rem(t, CORES)
    xpeer, sibling = f + 1 - 2 * x, t + 1 - 2 * c
    owner_t, owner_i = lax.div(f, R), lax.rem(f, R)
    to_self = owner_t == t
    mine = pl.ds(pl.multiple_of(c * kd, 128), kd)
    theirs = pl.ds(pl.multiple_of((1 - c) * kd, 128), kd)

    copy_a = pltpu.make_async_copy(a_ref, ga.at[f, :, mine], lsem.at[0])
    copy_q = pltpu.make_async_copy(q_ref, q, lsem.at[1])
    copy_a.start()
    copy_q.start()

    barrier = pltpu.get_barrier_semaphore()

    def greet(df, dt):
        pl.semaphore_signal(barrier, inc=1, device_id=(df, dt), device_id_type=MESH)

    @pl.when(z > 0)
    def _():
        greet(f - X, t)

    @pl.when(z < Z - 1)
    def _():
        greet(f + X, t)

    greet(xpeer, t)
    greet(f, sibling)

    def peer(o):
        return lax.rem(u + o, U)

    for o in range(1, U):
        greet(f, peer(o) * CORES + c)

    for i in range(R):
        @pl.loop(0, T)
        def _(t2):
            @pl.when(jnp.logical_not((t * R + i == f) & (t2 == t)))
            def _():
                greet(t * R + i, t2)

    waits = 2 + (U - 1) + F
    waits = waits + (z > 0).astype(jnp.int32) + (z < Z - 1).astype(jnp.int32)
    pl.semaphore_wait(barrier, waits - to_self.astype(jnp.int32))

    def shard(slot, j, lanes):
        return ga.at[slot, pl.ds(pl.multiple_of(j * cb, cb), cb), lanes]

    def gather_copy(zz, j, sem, df):
        slot = zz * X + x
        ref = shard(slot, j, mine)
        return pltpu.make_async_remote_copy(
            src_ref=ref, dst_ref=ref, send_sem=sem.at[zz, j],
            recv_sem=gr.at[slot, j], device_id=(df, t), device_id_type=MESH)

    def gather_recv(slot, j):
        ref = shard(slot, j, mine)
        pltpu.make_async_remote_copy(
            src_ref=ref, dst_ref=ref, send_sem=xs.at[0, 0],
            recv_sem=gr.at[slot, j], device_id=(xpeer, t), device_id_type=MESH).wait_recv()

    def share_copy(slot, j):
        ref = shard(slot, j, mine)
        return pltpu.make_async_remote_copy(
            src_ref=ref, dst_ref=ref, send_sem=ss.at[slot, j],
            recv_sem=sr.at[slot, j], device_id=(f, sibling), device_id_type=MESH)

    def share_recv(slot, j):
        ref = shard(slot, j, theirs)
        pltpu.make_async_remote_copy(
            src_ref=ref, dst_ref=ref, send_sem=ss.at[slot, j],
            recv_sem=sr.at[slot, j], device_id=(f, sibling), device_id_type=MESH).wait_recv()

    def forward(zz, j, act):
        @pl.when((zz <= z) & (z < Z - 1))
        def _():
            act(gather_copy(zz, j, up, f + X))

        @pl.when((zz >= z) & (z > 0))
        def _():
            act(gather_copy(zz, j, dn, f - X))

        act(gather_copy(zz, j, xs, xpeer))

    def sum_copy(slot, u2):
        return pltpu.make_async_remote_copy(
            src_ref=part.at[slot, pl.ds(pl.multiple_of(u2 * pb, pb), pb), :],
            dst_ref=rbuf.at[slot, u], send_sem=ts.at[slot, u2],
            recv_sem=tr.at[slot, u], device_id=(f, u2 * CORES + c), device_id_type=MESH)

    def sum_recv(slot, u2):
        pltpu.make_async_remote_copy(
            src_ref=rbuf.at[slot, u2], dst_ref=rbuf.at[slot, u2], send_sem=ts.at[slot, u2],
            recv_sem=tr.at[slot, u2], device_id=(f, u2 * CORES + c),
            device_id_type=MESH).wait_recv()

    def out_at(i, t2):
        rows = pl.ds(pl.multiple_of(lax.div(t2, CORES) * pb, pb), pb)
        half = lax.rem(t2, CORES)
        if aligned:
            return out_ref.at[rows, pl.ds(pl.multiple_of(i * hb + half * hh, 128), hh)]
        return out_ref.at[i * CORES + half, rows, :]

    def fin_remote(slot):
        return pltpu.make_async_remote_copy(
            src_ref=fin.at[slot], dst_ref=out_at(owner_i, t), send_sem=fs.at[slot],
            recv_sem=fr.at[owner_i, t], device_id=(slot, owner_t), device_id_type=MESH)

    def fin_local():
        return pltpu.make_async_copy(fin.at[f], out_at(owner_i, t), lsem.at[2])

    def multiply(slot):
        for j in range(CHUNKS):
            share_recv(slot, j)
        for lo in range(0, hh, 256):
            n = min(256, hh - lo)
            prod = lax.dot_general(ga[slot], w[lo:lo + n, :], (((1,), (1,)), ((), ())),
                                   preferred_element_type=jnp.float32)
            tile[:, lo:lo + n] = prod
            part[slot, :, lo:lo + n] = prod.astype(jnp.bfloat16)
        for o in range(1, U):
            sum_copy(slot, peer(o)).start()
        acc[slot] = tile[pl.ds(pl.multiple_of(u * pb, pb), pb), :]

    def add_up(slot):
        for o in range(1, U):
            sum_recv(slot, peer(o))
        total = acc[slot]
        for o in range(1, U):
            total = total + rbuf[slot, peer(o)].astype(jnp.float32)
        fin[slot] = total.astype(jnp.bfloat16)
        own = to_self & (slot == f)

        @pl.when(own)
        def _():
            fin_local().start()

        @pl.when(jnp.logical_not(own))
        def _():
            fin_remote(slot).start()

    def start(copy):
        copy.start()

    copy_a.wait()
    for j in range(CHUNKS):
        forward(z, j, start)
    for j in range(CHUNKS):
        share_copy(f, j).start()
    copy_q.wait()

    rows = math.gcd(hh, BLOCK)
    other = (1 - c) * hh
    give = pltpu.make_async_remote_copy(
        src_ref=q.at[pl.ds(pl.multiple_of(other, rows), hh), :], dst_ref=w.at[:, mine],
        send_sem=wsem.at[0], recv_sem=wsem.at[1], device_id=(f, sibling), device_id_type=MESH)

    def scaled(r):
        at = pl.ds(pl.multiple_of(r, rows), rows)
        return (q[at, :].astype(jnp.float32)
                * s_ref[pl.ds(lax.div(r, BLOCK), 1), :]).astype(jnp.bfloat16)

    @pl.loop(0, hh // rows)
    def _(b):
        r = other + b * rows
        q[pl.ds(pl.multiple_of(r, rows), rows), :] = scaled(r)

    give.start()

    @pl.loop(0, hh // rows)
    def _(b):
        w[pl.ds(pl.multiple_of(b * rows, rows), rows), mine] = scaled(c * hh + b * rows)

    pltpu.make_async_remote_copy(
        src_ref=q.at[pl.ds(pl.multiple_of(other, rows), hh), :], dst_ref=w.at[:, theirs],
        send_sem=wsem.at[0], recv_sem=wsem.at[1], device_id=(f, sibling),
        device_id_type=MESH).wait_recv()

    steps = 2 * Z - 1

    def when_valid(k, body):
        d = lax.div(k + 1, 2)
        zz = z + d * (1 - 2 * lax.rem(k, 2))

        @pl.when((k >= 0) & (k < steps) & (zz >= 0) & (zz < Z))
        def _():
            body(zz)

    def own_column(zz):
        slot = zz * X + x

        @pl.when(zz != z)
        def _():
            for j in range(CHUNKS):
                gather_recv(slot, j)
                forward(zz, j, start)
                share_copy(slot, j).start()

        multiply(slot)

    def other_column(zz):
        slot = zz * X + 1 - x
        for j in range(CHUNKS):
            gather_recv(slot, j)
            share_copy(slot, j).start()
        multiply(slot)

    @pl.loop(0, steps + LAG_X + LAG_SUM)
    def _(i):
        when_valid(i, own_column)
        when_valid(i - LAG_X, other_column)
        when_valid(i - LAG_SUM, lambda zz: add_up(zz * X + x))
        when_valid(i - LAG_X - LAG_SUM, lambda zz: add_up(zz * X + 1 - x))

    give.wait_send()

    @pl.loop(0, Z)
    def _(zz):
        for j in range(CHUNKS):
            forward(zz, j, lambda copy: copy.wait_send())

    @pl.loop(0, F)
    def _(slot):
        for j in range(CHUNKS):
            share_copy(slot, j).wait_send()
        for o in range(1, U):
            sum_copy(slot, peer(o)).wait_send()
        own = to_self & (slot == f)

        @pl.when(own)
        def _():
            fin_local().wait()

        @pl.when(jnp.logical_not(own))
        def _():
            fin_remote(slot).wait_send()

    for i in range(R):
        @pl.loop(0, T)
        def _(t2):
            @pl.when(jnp.logical_not((t * R + i == f) & (t2 == t)))
            def _():
                pltpu.make_async_remote_copy(
                    src_ref=fin.at[0], dst_ref=out_at(i, t2), send_sem=fs.at[0],
                    recv_sem=fr.at[i, t2], device_id=(t * R + i, t2),
                    device_id_type=MESH).wait_recv()


def hidden_gradient(F, T, grad_out, down_q, scales):
    R, Z, U = F // T, F // X, T // CORES
    tb, kd = grad_out.shape
    hb = down_q.shape[0]
    hh, pb = hb // CORES, tb // U
    aligned = hh % 128 == 0
    out_shape = (tb, R * hb) if aligned else (R * CORES, tb, hh)
    wide_scales = jnp.repeat(scales.astype(jnp.float32), BLOCK, axis=1)
    any_spec = pl.BlockSpec(memory_space=pl.ANY)
    dma = pltpu.SemaphoreType.DMA
    out = pl.pallas_call(
        functools.partial(kernel, F, T, aligned),
        out_shape=jax.ShapeDtypeStruct(out_shape, jnp.bfloat16),
        in_specs=[any_spec, any_spec, pl.BlockSpec(memory_space=pltpu.VMEM)],
        out_specs=any_spec,
        scratch_shapes=[
            pltpu.VMEM((F, tb, CORES * kd), jnp.bfloat16),
            pltpu.VMEM((hb, kd), jnp.bfloat16),
            pltpu.VMEM((hh, CORES * kd), jnp.bfloat16),
            pltpu.VMEM((F, tb, hh), jnp.bfloat16),
            pltpu.VMEM((tb, hh), jnp.float32),
            pltpu.VMEM((F, pb, hh), jnp.float32),
            pltpu.VMEM((F, U, pb, hh), jnp.bfloat16),
            pltpu.VMEM((F, pb, hh), jnp.bfloat16),
            dma((3,)),
            dma((2,)),
            dma((F, CHUNKS)),
            dma((Z, CHUNKS)),
            dma((Z, CHUNKS)),
            dma((Z, CHUNKS)),
            dma((F, CHUNKS)),
            dma((F, CHUNKS)),
            dma((F, U)),
            dma((F, U)),
            dma((F,)),
            dma((R, T)),
        ],
        compiler_params=pltpu.CompilerParams(
            collective_id=0, has_side_effects=True, vmem_limit_bytes=58 * 2**20),
        cost_estimate=pl.CostEstimate(
            flops=2 * F * tb * kd * hb, bytes_accessed=2 * hb * (kd + R * tb),
            transcendentals=0),
    )(grad_out, down_q, wide_scales)
    if aligned:
        return out
    return out.transpose(1, 0, 2).reshape(tb, R * hb)


def on_device(F, T, grad_out, down_q, scales, gate_act, up_act):
    grad_hidden = hidden_gradient(F, T, grad_out, down_q, scales).astype(jnp.float32)
    gate_val = gate_act.astype(jnp.float32)
    sigmoid_gate = jax.nn.sigmoid(gate_val)
    grad_up = (grad_hidden * gate_val * sigmoid_gate).astype(jnp.bfloat16)
    slope = sigmoid_gate * (1.0 + gate_val * (1.0 - sigmoid_gate))
    grad_gate = (grad_hidden * up_act.astype(jnp.float32) * slope).astype(jnp.bfloat16)
    return (grad_gate, grad_up)


def solution(mesh):
    F, T = mesh.shape["fsdp"], mesh.shape["tp"]
    spec = P("fsdp", "tp")
    return jax.shard_map(
        functools.partial(on_device, F, T),
        mesh=mesh, in_specs=(spec,) * 5, out_specs=(spec, spec), check_vma=False)
```

time: 149 us -> 140 us (0.940); the launches traced: 149 us -> 138 us
  Pallas kernels: 142 us -> 131 us
    pallas_call x1, Pallas kernels: 142 us -> 131 us  [hidden_gradient(): pl.pallas_call(functools.partial(kernel, F, T, aligned), out_shape=jax.Sh...]
where the time goes in v3:
time: 140 us; the launch traced here: 138 us
  Pallas kernels  131 us (94%)
  other arithmetic  4.33 us (3%)
  local copies, waits for them, and re-layouts  1.49 us (1%)
    pallas_call x1, Pallas kernels, hidden_gradient(): pl.pallas_call(functools.partial(kernel, F, T, aligned), out_shape=jax.Sh...  131 us
    convert_element_type x1, other arithmetic, on_device(): grad_up = (grad_hidden * gate_val * sigmoid_gate).astype(jnp.bfloat16)  4.33 us

profile of v3, /device:TPU:24, one launch (start us, length us, event | category | flops | bytes accessed | tf_op | source)
XLA Modules:
  0.0 137.6 jit_solution(9967963356695014954)
XLA Ops:
  0.6 0.8 broadcast_in_dim.3
  1.4 0.7 copy.7
  2.1 0.0 copy-start
  2.1 0.0 copy-start.1
  2.1 131.1 %shard_map.68 = bf16[256,3584]{1,0:T(8,128)(2,1)} custom-call(bf16[256,2048]{1,0:T(8,128)(2,1)} %a_ref.1, bf16[1792,2048]{1,0:T(8,128)(2,1)} %q_ref.1, f32[14,2048]{1,0:T(8,128)} %bitcast.4), custom_call_target="tpu_custom_call" | custom-call | flops 15032385536 | bytes 9175040 | tf_op jit(solution)/shard_map/pallas_call | solution.py:287
  133.3 0.0 copy-done
  133.3 0.0 copy-done.1
  133.3 4.3 %fusion.8 = (bf16[256,3584]{1,0:T(8,128)(2,1)}, bf16[256,3584]{1,0:T(8,128)(2,1)}) fusion(bf16[256,3584]{1,0:T(8,128)(2,1)S(1)} %copy-done, bf16[256,3584]{1,0:T(8,128)(2,1)} %shard_map.68, bf16[256,3584]{1,0:T(8,128)(2,1)S(1)} %copy-done.1), kind=kLoop, calls=%fused_computation.12 | loop fusion | flops 14680064 | bytes 9175040 | tf_op jit(solution)/shard_map/convert_element_type | solution.py:329
  (1 shorter events, 0.0 us)
Async XLA Ops:
  2.1 131.1 %copy-start = (bf16[256,3584]{1,0:T(8,128)(2,1)S(1)}, bf16[256,3584]{1,0:T(8,128)(2,1)}, u32[]{:S(2)}) copy-start(bf16[256,3584]{1,0:T(8,128)(2,1)} %param.8) | copy-start | bytes 5505028
  2.1 131.1 %copy-start.1 = (bf16[256,3584]{1,0:T(8,128)(2,1)S(1)}, bf16[256,3584]{1,0:T(8,128)(2,1)}, u32[]{:S(2)}) copy-start(bf16[256,3584]{1,0:T(8,128)(2,1)} %param.9) | copy-start | bytes 5505028

commit v4 on v3

--- a/solution.py
+++ b/solution.py
@@ -157,6 +157,8 @@
         for o in range(1, U):
             total = total + rbuf[slot, peer(o)].astype(jnp.float32)
         fin[slot] = total.astype(jnp.bfloat16)
+
+    def send_sum(slot):
         own = to_self & (slot == f)
 
         @pl.when(own)
@@ -206,15 +208,27 @@
 
     steps = 2 * Z - 1
 
+    below, above = z, Z - 1 - z
+    last = jnp.where(above >= below, 2 * above, 2 * below - 1)
+    near = (below == above) | (below == above + 1)
+    before_last = last - jnp.where(near, 1, 2)
+
     def when_valid(k, body):
         d = lax.div(k + 1, 2)
         zz = z + d * (1 - 2 * lax.rem(k, 2))
 
         @pl.when((k >= 0) & (k < steps) & (zz >= 0) & (zz < Z))
         def _():
-            body(zz)
-
-    def own_column(zz):
+            body(zz, k)
+
+    def send_held(column):
+        @pl.loop(0, steps)
+        def _(k):
+            @pl.when(k + LAG_SUM < last)
+            def _():
+                when_valid(k, lambda zz, _: send_sum(zz * X + column))
+
+    def own_column(zz, k):
         slot = zz * X + x
 
         @pl.when(zz != z)
@@ -226,19 +240,38 @@
 
         multiply(slot)
 
-    def other_column(zz):
+    def other_column(zz, k):
         slot = zz * X + 1 - x
         for j in range(CHUNKS):
             gather_recv(slot, j)
             share_copy(slot, j).start()
+
+        @pl.when(k == before_last)
+        def _():
+            send_held(x)
+
+        @pl.when(k == last)
+        def _():
+            send_held(1 - x)
+
         multiply(slot)
+
+    def sum_column(column):
+        def body(zz, k):
+            add_up(zz * X + column)
+
+            @pl.when(k + LAG_SUM >= last)
+            def _():
+                send_sum(zz * X + column)
+
+        return body
 
     @pl.loop(0, steps + LAG_X + LAG_SUM)
     def _(i):
         when_valid(i, own_column)
         when_valid(i - LAG_X, other_column)
-        when_valid(i - LAG_SUM, lambda zz: add_up(zz * X + x))
-        when_valid(i - LAG_X - LAG_SUM, lambda zz: add_up(zz * X + 1 - x))
+        when_valid(i - LAG_SUM, sum_column(x))
+        when_valid(i - LAG_X - LAG_SUM, sum_column(1 - x))
 
     give.wait_send()
 

time: 140 us -> 137 us (0.979)
  the two profiles are of different devices: /device:TPU:24 before, /device:TPU:25 now
where the time goes in v4:
time: 137 us; the launch traced here: 136 us
  Pallas kernels  130 us (95%)
  other arithmetic  4.33 us (3%)
  local copies, waits for them, and re-layouts  1.49 us (1%)
    pallas_call x1, Pallas kernels, hidden_gradient(): pl.pallas_call(functools.partial(kernel, F, T, aligned), out_shape=jax.Sh...  130 us
    convert_element_type x1, other arithmetic, on_device(): grad_up = (grad_hidden * gate_val * sigmoid_gate).astype(jnp.bfloat16)  4.33 us

profile of v4, /device:TPU:25, one launch (start us, length us, event | category | flops | bytes accessed | tf_op | source)
XLA Modules:
  0.0 136.4 jit_solution(12208331568402685675)
XLA Ops:
  0.6 0.8 broadcast_in_dim.3
  1.4 0.7 copy.7
  2.1 0.0 copy-start
  2.1 0.0 copy-start.1
  2.1 129.9 %shard_map.68 = bf16[256,3584]{1,0:T(8,128)(2,1)} custom-call(bf16[256,2048]{1,0:T(8,128)(2,1)} %a_ref.1, bf16[1792,2048]{1,0:T(8,128)(2,1)} %q_ref.1, f32[14,2048]{1,0:T(8,128)} %bitcast.4), custom_call_target="tpu_custom_call" | custom-call | flops 15032385536 | bytes 9175040 | tf_op jit(solution)/shard_map/pallas_call | solution.py:320
  132.0 0.0 copy-done
  132.1 0.0 copy-done.1
  132.1 4.3 %fusion.8 = (bf16[256,3584]{1,0:T(8,128)(2,1)}, bf16[256,3584]{1,0:T(8,128)(2,1)}) fusion(bf16[256,3584]{1,0:T(8,128)(2,1)S(1)} %copy-done, bf16[256,3584]{1,0:T(8,128)(2,1)} %shard_map.68, bf16[256,3584]{1,0:T(8,128)(2,1)S(1)} %copy-done.1), kind=kLoop, calls=%fused_computation.12 | loop fusion | flops 14680064 | bytes 9175040 | tf_op jit(solution)/shard_map/convert_element_type | solution.py:362
  (1 shorter events, 0.0 us)
Async XLA Ops:
  2.1 129.9 %copy-start = (bf16[256,3584]{1,0:T(8,128)(2,1)S(1)}, bf16[256,3584]{1,0:T(8,128)(2,1)}, u32[]{:S(2)}) copy-start(bf16[256,3584]{1,0:T(8,128)(2,1)} %param.8) | copy-start | bytes 5505028
  2.1 129.9 %copy-start.1 = (bf16[256,3584]{1,0:T(8,128)(2,1)S(1)}, bf16[256,3584]{1,0:T(8,128)(2,1)}, u32[]{:S(2)}) copy-start(bf16[256,3584]{1,0:T(8,128)(2,1)} %param.9) | copy-start | bytes 5505028

commit v5 on v4

--- a/solution.py
+++ b/solution.py
@@ -23,7 +23,8 @@
     tb, kd = a_ref.shape
     hb = q_ref.shape[0]
     hh = hb // CORES
-    pb, cb = tb // U, tb // CHUNKS
+    cb = tb // CHUNKS
+    pb = cb // U
     f, t = lax.axis_index("fsdp"), lax.axis_index("tp")
     z, x = lax.div(f, X), lax.rem(f, X)
     u, c = lax.div(t, CORES), lax.rem(t, CORES)
@@ -110,64 +111,68 @@
 
         act(gather_copy(zz, j, xs, xpeer))
 
-    def sum_copy(slot, u2):
+    def piece(j, u2):
+        return pl.ds(pl.multiple_of(j * cb + u2 * pb, pb), pb)
+
+    def sum_copy(slot, j, u2):
         return pltpu.make_async_remote_copy(
-            src_ref=part.at[slot, pl.ds(pl.multiple_of(u2 * pb, pb), pb), :],
-            dst_ref=rbuf.at[slot, u], send_sem=ts.at[slot, u2],
-            recv_sem=tr.at[slot, u], device_id=(f, u2 * CORES + c), device_id_type=MESH)
-
-    def sum_recv(slot, u2):
+            src_ref=part.at[slot, piece(j, u2), :], dst_ref=rbuf.at[slot, j, u],
+            send_sem=ts.at[slot, j, u2], recv_sem=tr.at[slot, j, u],
+            device_id=(f, u2 * CORES + c), device_id_type=MESH)
+
+    def sum_recv(slot, j, u2):
+        ref = rbuf.at[slot, j, u2]
         pltpu.make_async_remote_copy(
-            src_ref=rbuf.at[slot, u2], dst_ref=rbuf.at[slot, u2], send_sem=ts.at[slot, u2],
-            recv_sem=tr.at[slot, u2], device_id=(f, u2 * CORES + c),
+            src_ref=ref, dst_ref=ref, send_sem=ts.at[slot, j, u2],
+            recv_sem=tr.at[slot, j, u2], device_id=(f, u2 * CORES + c),
             device_id_type=MESH).wait_recv()
 
-    def out_at(i, t2):
-        rows = pl.ds(pl.multiple_of(lax.div(t2, CORES) * pb, pb), pb)
+    def out_at(i, j, t2):
+        rows = piece(j, lax.div(t2, CORES))
         half = lax.rem(t2, CORES)
         if aligned:
             return out_ref.at[rows, pl.ds(pl.multiple_of(i * hb + half * hh, 128), hh)]
         return out_ref.at[i * CORES + half, rows, :]
 
-    def fin_remote(slot):
+    def fin_remote(slot, j):
         return pltpu.make_async_remote_copy(
-            src_ref=fin.at[slot], dst_ref=out_at(owner_i, t), send_sem=fs.at[slot],
-            recv_sem=fr.at[owner_i, t], device_id=(slot, owner_t), device_id_type=MESH)
-
-    def fin_local():
-        return pltpu.make_async_copy(fin.at[f], out_at(owner_i, t), lsem.at[2])
-
-    def multiply(slot):
-        for j in range(CHUNKS):
-            share_recv(slot, j)
+            src_ref=fin.at[slot, j], dst_ref=out_at(owner_i, j, t), send_sem=fs.at[slot, j],
+            recv_sem=fr.at[owner_i, j, t], device_id=(slot, owner_t), device_id_type=MESH)
+
+    def fin_local(j):
+        return pltpu.make_async_copy(fin.at[f, j], out_at(owner_i, j, t), lsem.at[2 + j])
+
+    def multiply(slot, j):
+        share_recv(slot, j)
+        rows = pl.ds(j * cb, cb)
         for lo in range(0, hh, 256):
             n = min(256, hh - lo)
-            prod = lax.dot_general(ga[slot], w[lo:lo + n, :], (((1,), (1,)), ((), ())),
+            prod = lax.dot_general(ga[slot, rows, :], w[lo:lo + n, :], (((1,), (1,)), ((), ())),
                                    preferred_element_type=jnp.float32)
             tile[:, lo:lo + n] = prod
-            part[slot, :, lo:lo + n] = prod.astype(jnp.bfloat16)
+            part[slot, rows, lo:lo + n] = prod.astype(jnp.bfloat16)
         for o in range(1, U):
-            sum_copy(slot, peer(o)).start()
-        acc[slot] = tile[pl.ds(pl.multiple_of(u * pb, pb), pb), :]
-
-    def add_up(slot):
+            sum_copy(slot, j, peer(o)).start()
+        acc[slot, j] = tile[pl.ds(pl.multiple_of(u * pb, pb), pb), :]
+
+    def add_up(slot, j):
         for o in range(1, U):
-            sum_recv(slot, peer(o))
-        total = acc[slot]
+            sum_recv(slot, j, peer(o))
+        total = acc[slot, j]
         for o in range(1, U):
-            total = total + rbuf[slot, peer(o)].astype(jnp.float32)
-        fin[slot] = total.astype(jnp.bfloat16)
-
-    def send_sum(slot):
+            total = total + rbuf[slot, j, peer(o)].astype(jnp.float32)
+        fin[slot, j] = total.astype(jnp.bfloat16)
+
+    def send_sum(slot, j):
         own = to_self & (slot == f)
 
         @pl.when(own)
         def _():
-            fin_local().start()
+            fin_local(j).start()
 
         @pl.when(jnp.logical_not(own))
         def _():
-            fin_remote(slot).start()
+            fin_remote(slot, j).start()
 
     def start(copy):
         copy.start()
@@ -222,56 +227,75 @@
             body(zz, k)
 
     def send_held(column):
+        def body(zz, _):
+            for j in range(CHUNKS):
+                send_sum(zz * X + column, j)
+
         @pl.loop(0, steps)
         def _(k):
             @pl.when(k + LAG_SUM < last)
             def _():
-                when_valid(k, lambda zz, _: send_sum(zz * X + column))
+                when_valid(k, body)
 
     def own_column(zz, k):
         slot = zz * X + x
-
-        @pl.when(zz != z)
-        def _():
-            for j in range(CHUNKS):
+        for j in range(CHUNKS):
+            @pl.when(zz != z)
+            def _():
                 gather_recv(slot, j)
                 forward(zz, j, start)
                 share_copy(slot, j).start()
 
-        multiply(slot)
+            multiply(slot, j)
 
     def other_column(zz, k):
         slot = zz * X + 1 - x
         for j in range(CHUNKS):
             gather_recv(slot, j)
             share_copy(slot, j).start()
-
-        @pl.when(k == before_last)
-        def _():
-            send_held(x)
-
-        @pl.when(k == last)
-        def _():
-            send_held(1 - x)
-
-        multiply(slot)
-
-    def sum_column(column):
-        def body(zz, k):
-            add_up(zz * X + column)
+            if j == 0:
+                @pl.when(k == before_last)
+                def _():
+                    send_held(x)
+            else:
+                add_up(slot, j - 1)
+
+                @pl.when(k == last)
+                def _():
+                    if j == 1:
+                        send_held(1 - x)
+                    send_sum(slot, j - 1)
+
+            multiply(slot, j)
+
+    def sum_own(zz, k):
+        slot = zz * X + x
+        for j in range(CHUNKS):
+            add_up(slot, j)
 
             @pl.when(k + LAG_SUM >= last)
             def _():
-                send_sum(zz * X + column)
-
-        return body
+                send_sum(slot, j)
+
+    def sum_other(zz, k):
+        slot = zz * X + 1 - x
+        add_up(slot, CHUNKS - 1)
+
+        @pl.when((k + LAG_SUM >= last) & (k < last))
+        def _():
+            for j in range(CHUNKS - 1):
+                send_sum(slot, j)
+
+        @pl.when(k + LAG_SUM >= last)
+        def _():
+            send_sum(slot, CHUNKS - 1)
 
     @pl.loop(0, steps + LAG_X + LAG_SUM)
     def _(i):
         when_valid(i, own_column)
         when_valid(i - LAG_X, other_column)
-        when_valid(i - LAG_SUM, sum_column(x))
-        when_valid(i - LAG_X - LAG_SUM, sum_column(1 - x))
+        when_valid(i - LAG_SUM, sum_own)
+        when_valid(i - LAG_X - LAG_SUM, sum_other)
 
     give.wait_send()
 
@@ -284,34 +308,37 @@
     def _(slot):
         for j in range(CHUNKS):
             share_copy(slot, j).wait_send()
-        for o in range(1, U):
-            sum_copy(slot, peer(o)).wait_send()
         own = to_self & (slot == f)
-
-        @pl.when(own)
-        def _():
-            fin_local().wait()
-
-        @pl.when(jnp.logical_not(own))
-        def _():
-            fin_remote(slot).wait_send()
+        for j in range(CHUNKS):
+            for o in range(1, U):
+                sum_copy(slot, j, peer(o)).wait_send()
+
+            @pl.when(own)
+            def _():
+                fin_local(j).wait()
+
+            @pl.when(jnp.logical_not(own))
+            def _():
+                fin_remote(slot, j).wait_send()
 
     for i in range(R):
         @pl.loop(0, T)
         def _(t2):
             @pl.when(jnp.logical_not((t * R + i == f) & (t2 == t)))
             def _():
-                pltpu.make_async_remote_copy(
-                    src_ref=fin.at[0], dst_ref=out_at(i, t2), send_sem=fs.at[0],
-                    recv_sem=fr.at[i, t2], device_id=(t * R + i, t2),
-                    device_id_type=MESH).wait_recv()
+                for j in range(CHUNKS):
+                    pltpu.make_async_remote_copy(
+                        src_ref=fin.at[0, 0], dst_ref=out_at(i, j, t2), send_sem=fs.at[0, 0],
+                        recv_sem=fr.at[i, j, t2], device_id=(t * R + i, t2),
+                        device_id_type=MESH).wait_recv()
 
 
 def hidden_gradient(F, T, grad_out, down_q, scales):
     R, Z, U = F // T, F // X, T // CORES
     tb, kd = grad_out.shape
     hb = down_q.shape[0]
-    hh, pb = hb // CORES, tb // U
+    hh, cb = hb // CORES, tb // CHUNKS
+    pb = cb // U
     aligned = hh % 128 == 0
     out_shape = (tb, R * hb) if aligned else (R * CORES, tb, hh)
     wide_scales = jnp.repeat(scales.astype(jnp.float32), BLOCK, axis=1)
@@ -327,11 +354,11 @@
             pltpu.VMEM((hb, kd), jnp.bfloat16),
             pltpu.VMEM((hh, CORES * kd), jnp.bfloat16),
             pltpu.VMEM((F, tb, hh), jnp.bfloat16),
-            pltpu.VMEM((tb, hh), jnp.float32),
-            pltpu.VMEM((F, pb, hh), jnp.float32),
-            pltpu.VMEM((F, U, pb, hh), jnp.bfloat16),
-            pltpu.VMEM((F, pb, hh), jnp.bfloat16),
-            dma((3,)),
+            pltpu.VMEM((cb, hh), jnp.float32),
+            pltpu.VMEM((F, CHUNKS, pb, hh), jnp.float32),
+            pltpu.VMEM((F, CHUNKS, U, pb, hh), jnp.bfloat16),
+            pltpu.VMEM((F, CHUNKS, pb, hh), jnp.bfloat16),
+            dma((2 + CHUNKS,)),
             dma((2,)),
             dma((F, CHUNKS)),
             dma((Z, CHUNKS)),
@@ -339,10 +366,10 @@
             dma((Z, CHUNKS)),
             dma((F, CHUNKS)),
             dma((F, CHUNKS)),
-            dma((F, U)),
-            dma((F, U)),
-            dma((F,)),
-            dma((R, T)),
+            dma((F, CHUNKS, U)),
+            dma((F, CHUNKS, U)),
+            dma((F, CHUNKS)),
+            dma((R, CHUNKS, T)),
         ],
         compiler_params=pltpu.CompilerParams(
             collective_id=0, has_side_effects=True, vmem_limit_bytes=58 * 2**20),

time: 137 us -> 146 us (1.066)
  the two profiles are of different devices: /device:TPU:25 before, /device:TPU:24 now
where the time goes in v5:
time: 146 us
  Pallas kernels  139 us (95%)
  other arithmetic  4.33 us (3%)
  local copies, waits for them, and re-layouts  1.49 us (1%)
    pallas_call x1, Pallas kernels, hidden_gradient(): pl.pallas_call(functools.partial(kernel, F, T, aligned), out_shape=jax.Sh...  139 us
    convert_element_type x1, other arithmetic, on_device(): grad_up = (grad_hidden * gate_val * sigmoid_gate).astype(jnp.bfloat16)  4.33 us

profile of v5, /device:TPU:24, one launch (start us, length us, event | category | flops | bytes accessed | tf_op | source)
XLA Modules:
  0.0 145.8 jit_solution(13775811227787984036)
XLA Ops:
  0.6 0.8 broadcast_in_dim.3
  1.4 0.7 copy.7
  2.1 0.0 copy-start
  2.1 0.0 copy-start.1
  2.1 139.3 %shard_map.68 = bf16[256,3584]{1,0:T(8,128)(2,1)} custom-call(bf16[256,2048]{1,0:T(8,128)(2,1)} %a_ref.1, bf16[1792,2048]{1,0:T(8,128)(2,1)} %q_ref.1, f32[14,2048]{1,0:T(8,128)} %bitcast.4), custom_call_target="tpu_custom_call" | custom-call | flops 15032385536 | bytes 9175040 | tf_op jit(solution)/shard_map/pallas_call | solution.py:347
  141.4 0.0 copy-done
  141.5 0.0 copy-done.1
  141.5 4.3 %fusion.8 = (bf16[256,3584]{1,0:T(8,128)(2,1)}, bf16[256,3584]{1,0:T(8,128)(2,1)}) fusion(bf16[256,3584]{1,0:T(8,128)(2,1)S(1)} %copy-done, bf16[256,3584]{1,0:T(8,128)(2,1)} %shard_map.68, bf16[256,3584]{1,0:T(8,128)(2,1)S(1)} %copy-done.1), kind=kLoop, calls=%fused_computation.12 | loop fusion | flops 14680064 | bytes 9175040 | tf_op jit(solution)/shard_map/convert_element_type | solution.py:389
  (1 shorter events, 0.0 us)
Async XLA Ops:
  2.1 139.3 %copy-start = (bf16[256,3584]{1,0:T(8,128)(2,1)S(1)}, bf16[256,3584]{1,0:T(8,128)(2,1)}, u32[]{:S(2)}) copy-start(bf16[256,3584]{1,0:T(8,128)(2,1)} %param.8) | copy-start | bytes 5505028
  2.1 139.3 %copy-start.1 = (bf16[256,3584]{1,0:T(8,128)(2,1)S(1)}, bf16[256,3584]{1,0:T(8,128)(2,1)}, u32[]{:S(2)}) copy-start(bf16[256,3584]{1,0:T(8,128)(2,1)} %param.9) | copy-start | bytes 5505028

commit v6 on v5

--- a/solution.py
+++ b/solution.py
@@ -142,18 +142,21 @@
     def fin_local(j):
         return pltpu.make_async_copy(fin.at[f, j], out_at(owner_i, j, t), lsem.at[2 + j])
 
-    def multiply(slot, j):
-        share_recv(slot, j)
-        rows = pl.ds(j * cb, cb)
+    def multiply(slot, first, count):
+        for j in range(first, first + count):
+            share_recv(slot, j)
+        rows = pl.ds(first * cb, count * cb)
         for lo in range(0, hh, 256):
             n = min(256, hh - lo)
             prod = lax.dot_general(ga[slot, rows, :], w[lo:lo + n, :], (((1,), (1,)), ((), ())),
                                    preferred_element_type=jnp.float32)
-            tile[:, lo:lo + n] = prod
+            tile[rows, lo:lo + n] = prod
             part[slot, rows, lo:lo + n] = prod.astype(jnp.bfloat16)
-        for o in range(1, U):
-            sum_copy(slot, j, peer(o)).start()
-        acc[slot, j] = tile[pl.ds(pl.multiple_of(u * pb, pb), pb), :]
+        for j in range(first, first + count):
+            for o in range(1, U):
+                sum_copy(slot, j, peer(o)).start()
+        for j in range(first, first + count):
+            acc[slot, j] = tile[piece(j, u), :]
 
     def add_up(slot, j):
         for o in range(1, U):
@@ -239,34 +242,43 @@
 
     def own_column(zz, k):
         slot = zz * X + x
-        for j in range(CHUNKS):
-            @pl.when(zz != z)
-            def _():
+
+        @pl.when(zz != z)
+        def _():
+            for j in range(CHUNKS):
                 gather_recv(slot, j)
                 forward(zz, j, start)
                 share_copy(slot, j).start()
 
-            multiply(slot, j)
+        multiply(slot, 0, CHUNKS)
 
     def other_column(zz, k):
         slot = zz * X + 1 - x
-        for j in range(CHUNKS):
-            gather_recv(slot, j)
-            share_copy(slot, j).start()
-            if j == 0:
-                @pl.when(k == before_last)
-                def _():
-                    send_held(x)
-            else:
-                add_up(slot, j - 1)
-
-                @pl.when(k == last)
-                def _():
-                    if j == 1:
-                        send_held(1 - x)
+
+        @pl.when(k < last)
+        def _():
+            for j in range(CHUNKS):
+                gather_recv(slot, j)
+                share_copy(slot, j).start()
+
+            @pl.when(k == before_last)
+            def _():
+                send_held(x)
+
+            multiply(slot, 0, CHUNKS)
+
+        @pl.when(k == last)
+        def _():
+            for j in range(CHUNKS):
+                gather_recv(slot, j)
+                share_copy(slot, j).start()
+                if j > 0:
+                    add_up(slot, j - 1)
+                if j == CHUNKS - 1:
+                    send_held(1 - x)
+                if j > 0:
                     send_sum(slot, j - 1)
-
-            multiply(slot, j)
+                multiply(slot, j, 1)
 
     def sum_own(zz, k):
         slot = zz * X + x
@@ -279,12 +291,16 @@
 
     def sum_other(zz, k):
         slot = zz * X + 1 - x
+        for j in range(CHUNKS - 1):
+            @pl.when(k < last)
+            def _():
+                add_up(slot, j)
+
+                @pl.when(k + LAG_SUM >= last)
+                def _():
+                    send_sum(slot, j)
+
         add_up(slot, CHUNKS - 1)
-
-        @pl.when((k + LAG_SUM >= last) & (k < last))
-        def _():
-            for j in range(CHUNKS - 1):
-                send_sum(slot, j)
 
         @pl.when(k + LAG_SUM >= last)
         def _():
@@ -293,9 +309,9 @@
     @pl.loop(0, steps + LAG_X + LAG_SUM)
     def _(i):
         when_valid(i, own_column)
+        when_valid(i - LAG_X - 1, sum_other)
         when_valid(i - LAG_X, other_column)
         when_valid(i - LAG_SUM, sum_own)
-        when_valid(i - LAG_X - LAG_SUM, sum_other)
 
     give.wait_send()
 
@@ -354,7 +370,7 @@
             pltpu.VMEM((hb, kd), jnp.bfloat16),
             pltpu.VMEM((hh, CORES * kd), jnp.bfloat16),
             pltpu.VMEM((F, tb, hh), jnp.bfloat16),
-            pltpu.VMEM((cb, hh), jnp.float32),
+            pltpu.VMEM((tb, hh), jnp.float32),
             pltpu.VMEM((F, CHUNKS, pb, hh), jnp.float32),
             pltpu.VMEM((F, CHUNKS, U, pb, hh), jnp.bfloat16),
             pltpu.VMEM((F, CHUNKS, pb, hh), jnp.bfloat16),

time: 146 us -> 141 us (0.966); the launches traced: 146 us -> 138 us
  Pallas kernels: 139 us -> 132 us
    pallas_call x1, Pallas kernels: 139 us -> 132 us  [hidden_gradient(): pl.pallas_call(functools.partial(kernel, F, T, aligned), out_shape=jax.Sh...]
where the time goes in v6:
time: 141 us; the launch traced here: 138 us
  Pallas kernels  132 us (94%)
  other arithmetic  4.33 us (3%)
  local copies, waits for them, and re-layouts  1.49 us (1%)
    pallas_call x1, Pallas kernels, hidden_gradient(): pl.pallas_call(functools.partial(kernel, F, T, aligned), out_shape=jax.Sh...  132 us
    convert_element_type x1, other arithmetic, on_device(): grad_up = (grad_hidden * gate_val * sigmoid_gate).astype(jnp.bfloat16)  4.33 us

profile of v6, /device:TPU:24, one launch (start us, length us, event | category | flops | bytes accessed | tf_op | source)
XLA Modules:
  0.0 138.3 jit_solution(5774421403615266598)
XLA Ops:
  0.6 0.8 broadcast_in_dim.3
  1.4 0.7 copy.7
  2.1 0.0 copy-start
  2.1 0.0 copy-start.1
  2.1 131.8 %shard_map.68 = bf16[256,3584]{1,0:T(8,128)(2,1)} custom-call(bf16[256,2048]{1,0:T(8,128)(2,1)} %a_ref.1, bf16[1792,2048]{1,0:T(8,128)(2,1)} %q_ref.1, f32[14,2048]{1,0:T(8,128)} %bitcast.4), custom_call_target="tpu_custom_call" | custom-call | flops 15032385536 | bytes 9175040 | tf_op jit(solution)/shard_map/pallas_call | solution.py:363
  134.0 0.0 copy-done
  134.0 0.0 copy-done.1
  134.0 4.3 %fusion.8 = (bf16[256,3584]{1,0:T(8,128)(2,1)}, bf16[256,3584]{1,0:T(8,128)(2,1)}) fusion(bf16[256,3584]{1,0:T(8,128)(2,1)S(1)} %copy-done, bf16[256,3584]{1,0:T(8,128)(2,1)} %shard_map.68, bf16[256,3584]{1,0:T(8,128)(2,1)S(1)} %copy-done.1), kind=kLoop, calls=%fused_computation.12 | loop fusion | flops 14680064 | bytes 9175040 | tf_op jit(solution)/shard_map/convert_element_type | solution.py:405
  (1 shorter events, 0.0 us)
Async XLA Ops:
  2.1 131.8 %copy-start = (bf16[256,3584]{1,0:T(8,128)(2,1)S(1)}, bf16[256,3584]{1,0:T(8,128)(2,1)}, u32[]{:S(2)}) copy-start(bf16[256,3584]{1,0:T(8,128)(2,1)} %param.8) | copy-start | bytes 5505028
  2.1 131.8 %copy-start.1 = (bf16[256,3584]{1,0:T(8,128)(2,1)S(1)}, bf16[256,3584]{1,0:T(8,128)(2,1)}, u32[]{:S(2)}) copy-start(bf16[256,3584]{1,0:T(8,128)(2,1)} %param.9) | copy-start | bytes 5505028
